TPU v7x, 512 devices: a whole 4x8x8 slice. The times are simulated.
512 devices in a mesh: row: 32 (over y, z_lo), col: 16 (over x, z_hi, core).
Axes of the slice: x: 4, y: 8, z: 8 (z_hi: 2, z_lo: 4; z = z_hi * 4 + z_lo), core: 2. Of those that a mesh axis runs over, the one named last changes fastest.
Arguments:
- b_old: float32 [65536, 128], P('col'), may hold values from 0.2 to 2
- positions: float32 [3, 65536], P(None, 'col'), may hold values from -1 to 1
- angles: float32 [2, 65536], P(None, 'col'), may hold values from -3.140625 to 3.140625
- areas: float32 [65536], P('col'), may hold values from 0.00030517578 to 0.0045776367
- visible: int32 [128, 128], replicated, may hold values from 0 to 1
- assign: int32 [65536], P('col'), may hold values from 0 to 127, never falling along the last dimension, each value on 1 to 1024 neighbouring positions
- emission: float32 [65536, 128], P(('row', 'col')), may hold values from 0 to 1
- reflect: float32 [65536, 128], P(('row', 'col')), may hold values from 0.2 to 0.95
Outputs:
- b_new: float32 [65536, 128], P(('row', 'col'))
Inputs may be any that keep to these rules, and one draw needn't show every extreme that they name: assign never falls along the facets; every block holds 1 to 1024 facets.
All inputs are finite; a program needn't handle non-finite values.
Results may differ from a plain program's by a relative error of at most 0.0003.
Values sent between devices are 32-bit elements; how exact they have to be, the bound alone decides.
A program may use at most 64 MiB of HBM per device.

v0:
```python
import math

import jax
import jax.numpy as jnp
from jax import lax
from jax.sharding import PartitionSpec as P


def spread(block, axis, source):
    block = jnp.where(lax.axis_index(axis) == source, block, jnp.zeros_like(block))
    return lax.psum(block, axis)


def facet_normals(angles):
    azimuth = angles[0]
    elevation = angles[1]
    return jnp.stack(
        [
            jnp.cos(azimuth) * jnp.cos(elevation),
            jnp.sin(azimuth) * jnp.cos(elevation),
            jnp.sin(elevation),
        ]
    )


def view_tile(row_pos, row_nrm, col_pos, col_nrm, col_area, mask):
    along_x = col_pos[0][None, :] - row_pos[0][:, None]
    along_y = col_pos[1][None, :] - row_pos[1][:, None]
    along_z = col_pos[2][None, :] - row_pos[2][:, None]
    cos_row = (
        row_nrm[0][:, None] * along_x
        + row_nrm[1][:, None] * along_y
        + row_nrm[2][:, None] * along_z
    )
    cos_col = -(
        col_nrm[0][None, :] * along_x
        + col_nrm[1][None, :] * along_y
        + col_nrm[2][None, :] * along_z
    )
    dist_sq = (
        along_x * along_x + along_y * along_y + along_z * along_z + col_area[None, :] / math.pi
    )
    return (
        mask
        * jnp.maximum(cos_row, 0.0)
        * jnp.maximum(cos_col, 0.0)
        * col_area[None, :]
        / (math.pi * dist_sq * dist_sq)
    )


def unit_term(row_pos, row_nrm, row_ids, col_pos, col_nrm, col_area, col_ids, col_rad, vis_half):
    block_ids = jnp.arange(vis_half.shape[0], dtype=jnp.int32)
    onehot_row = (row_ids[:, None] == block_ids[None, :]).astype(jnp.bfloat16)
    onehot_col = (col_ids[:, None] == block_ids[None, :]).astype(jnp.bfloat16)
    seen_rows = jnp.dot(onehot_row, vis_half, preferred_element_type=jnp.float32).astype(
        jnp.bfloat16
    )
    mask = lax.dot_general(
        seen_rows, onehot_col, (((1,), (1,)), ((), ())), preferred_element_type=jnp.float32
    )
    tile = view_tile(row_pos, row_nrm, col_pos, col_nrm, col_area, mask)
    return jnp.dot(
        tile, col_rad, precision=lax.Precision.HIGHEST, preferred_element_type=jnp.float32
    )


def range_select(ids, tile_size, block_count):
    grouped = ids.reshape(ids.shape[0] // tile_size, tile_size)
    block_ids = jnp.arange(block_count, dtype=jnp.int32)
    lowest = grouped[:, 0]
    highest = grouped[:, tile_size - 1]
    return (
        (block_ids[None, :] >= lowest[:, None]) & (block_ids[None, :] <= highest[:, None])
    ).astype(jnp.float32)


def on_device(b_old, positions, angles, areas, visible, assign, emission, reflect):
    col_block = b_old.shape[0]
    band_count = b_old.shape[1]
    block_count = visible.shape[0]
    col_count = lax.axis_size("col")
    row_block = emission.shape[0] * col_count
    row_start = lax.axis_index("row") * row_block
    owner_col = row_start // col_block
    row_offset = row_start - owner_col * col_block
    got_pos, got_ang, got_ids = (
        spread(positions, "col", owner_col),
        spread(angles, "col", owner_col),
        spread(assign.astype(jnp.float32), "col", owner_col),
    )
    row_pos = lax.dynamic_slice_in_dim(got_pos, row_offset, row_block, 1)
    row_nrm = facet_normals(lax.dynamic_slice_in_dim(got_ang, row_offset, row_block, 1))
    row_ids = lax.dynamic_slice_in_dim(got_ids, row_offset, row_block, 0).astype(jnp.int32)
    vis_half = visible.astype(jnp.bfloat16)
    vis_full = visible.astype(jnp.float32)
    tile_rows = min(512, row_block)
    tile_cols = min(1024, col_block)
    col_rad, col_pos, col_ang, col_area, col_ids = (b_old, positions, angles, areas, assign)
    col_nrm = facet_normals(col_ang)
    units_rows = row_block // tile_rows
    units_cols = col_rad.shape[0] // tile_cols
    row_sel = range_select(row_ids, tile_rows, block_count)
    col_sel = range_select(col_ids, tile_cols, block_count)
    through = jnp.dot(
        row_sel, vis_full, precision=lax.Precision.HIGHEST, preferred_element_type=jnp.float32
    )
    pair_hits = lax.dot_general(
        through,
        col_sel,
        (((1,), (1,)), ((), ())),
        precision=lax.Precision.HIGHEST,
        preferred_element_type=jnp.float32,
    )
    live_flags = (pair_hits > 0.5).reshape(-1)

    def visit(which, partial_value):
        row_first = which // units_cols * tile_rows
        col_first = which % units_cols * tile_cols

        def work():
            return unit_term(
                lax.dynamic_slice_in_dim(row_pos, row_first, tile_rows, 1),
                lax.dynamic_slice_in_dim(row_nrm, row_first, tile_rows, 1),
                lax.dynamic_slice_in_dim(row_ids, row_first, tile_rows, 0),
                lax.dynamic_slice_in_dim(col_pos, col_first, tile_cols, 1),
                lax.dynamic_slice_in_dim(col_nrm, col_first, tile_cols, 1),
                lax.dynamic_slice_in_dim(col_area, col_first, tile_cols, 0),
                lax.dynamic_slice_in_dim(col_ids, col_first, tile_cols, 0),
                lax.dynamic_slice_in_dim(col_rad, col_first, tile_cols, 0),
                vis_half,
            )

        def skipped():
            return jnp.zeros((tile_rows, band_count), jnp.float32)

        contrib = lax.cond(live_flags[which], work, skipped)
        current = lax.dynamic_slice_in_dim(partial_value, row_first, tile_rows, 0)
        return lax.dynamic_update_slice_in_dim(partial_value, current + contrib, row_first, 0)

    partial_value = lax.fori_loop(
        0, units_rows * units_cols, visit, jnp.zeros((row_block, band_count), jnp.float32)
    )
    summed = lax.psum_scatter(partial_value, "col", scatter_dimension=0, tiled=True)
    return emission + reflect * summed


def solution(mesh):
    return jax.shard_map(
        on_device,
        mesh=mesh,
        in_specs=(
            P("col", None),
            P(None, "col"),
            P(None, "col"),
            P("col"),
            P(),
            P("col"),
            P(("row", "col"), None),
            P(("row", "col"), None),
        ),
        out_specs=P(("row", "col"), None),
        check_vma=False,
    )
```

profile of v0, /device:TPU:24, one launch (start us, length us, event | category | flops | bytes accessed | tf_op | source)
XLA Modules:
  0.0 455.7 jit_solution(18441230186433300155)
XLA Ops:
  7.8 1.3 convert_select_fusion
  9.9 1.8 cosine_multiply_fusion
  12.8 180.4 %all-reduce.3.cloned.1.call-done = (f32[4096]{0:T(1024)}, f32[2,4096]{1,0:T(2,128)}, f32[3,4096]{1,0:T(4,128)}) async-done(((f32[4096]{0:T(1024)}, f32[2,4096]{1,0:T(2,128)}, f32[3,4096]{1,0:T(4,128)}), (f32[4096]{0:T(1024)}, f32[2,4096]{1,0:T(2,128)}, f32[3,4096]{1,0:T(4,128)})) %all-reduce.3.cloned.1.call-update) | async-done | bytes 98320 | tf_op jit(solution)/shard_map/psum | solution.py:11
  194.1 1.0 fusion.40
  195.4 1.3 cosine_multiply_fusion.1
  196.7 1.4 pad_maximum_fusion.1
  198.2 109.0 %while.15 = (s32[]{:T(128)}, f32[2048,128]{1,0:T(8,128)S(1)}, pred[16]{0:T(512)(128)(4,1)S(1)}, s32[2048]{0:T(1024)S(1)}, bf16[128,128]{1,0:T(8,128)(2,1)S(1)}, ...) while((s32[]{:T(128)}, f32[2048,128]{1,0:T(8,128)S(1)}, ...), condition=%wide.region_6.7_spmd, body=%wide.region_3.6_spmd.sunk | while | flops 971310080 | bytes 5950101 | solution.py:141
  200.8 8.8 %conditional.2 = (f32[512,128]{1,0:T(8,128)S(1)}) conditional(s32[]{:T(128)} %bitcast.16, () %tuple.83, (s32[]{:T(128)}, s32[2048]{0:T(1024)S(1)}, bf16[128,128]{1,0:T(8,128)(2,1)S(1)}, s32[]{:T(128)}, s32[4096]{0:T(1024)}, /*index=5*/f32[3,2048]{1,0:T(4,128)S(1)}, f32[3,4096]{1,0:T(4,128)}, f32[3,2048]{1,0:T(4,128)}, f32[3,4096]{1,0:T(4,128)S(1)}, ...), branch_computations={%region_4.4_spmd, %region_5.5_spmd} | conditional | flops 971244544 | bytes 5163269 | solution.py:137
  202.2 0.9 constant_dynamic-slice_fusion
  203.9 0.9 constant_dynamic-slice_fusion.1
  204.8 4.8 %fusion.14 = f32[512,128]{1,0:T(8,128)S(1)} fusion(f32[512,1024]{1,0:T(8,128)S(1)} %fusion.16, f32[1024]{0:T(1024)S(1)} %get-tuple-element.470, f32[1024]{0:T(1024)S(1)} %get-tuple-element.471, f32[1024]{0:T(1024)S(1)} %bitcast.20, f32[1024]{0:T(1024)S(1)} %bitcast.21, f32[1024]{0:T(1024)S(1)} %bitcast.22, f32[512]{0:T(512)S(1)} %bitcast.26, ...), kind=kOutput, calls=%fused_computation.24 | convolution fusion | flops 819986432 | bytes 2928644 | tf_op jit(solution)/shard_map/while/body/eval_jaxpr/cond/branch_1_fun/dot_general | solution.py:63
  210.9 8.8 %conditional.2 = (f32[512,128]{1,0:T(8,128)S(1)}) conditional(s32[]{:T(128)} %bitcast.16, () %tuple.83, (s32[]{:T(128)}, s32[2048]{0:T(1024)S(1)}, bf16[128,128]{1,0:T(8,128)(2,1)S(1)}, s32[]{:T(128)}, s32[4096]{0:T(1024)}, /*index=5*/f32[3,2048]{1,0:T(4,128)S(1)}, f32[3,4096]{1,0:T(4,128)}, f32[3,2048]{1,0:T(4,128)}, f32[3,4096]{1,0:T(4,128)S(1)}, ...), branch_computations={%region_4.4_spmd, %region_5.5_spmd} | conditional | flops 971244544 | bytes 5163269 | solution.py:137
  212.3 0.9 constant_dynamic-slice_fusion
  214.0 0.9 constant_dynamic-slice_fusion.1
  214.9 4.8 %fusion.14 = f32[512,128]{1,0:T(8,128)S(1)} fusion(f32[512,1024]{1,0:T(8,128)S(1)} %fusion.16, f32[1024]{0:T(1024)S(1)} %get-tuple-element.470, f32[1024]{0:T(1024)S(1)} %get-tuple-element.471, f32[1024]{0:T(1024)S(1)} %bitcast.20, f32[1024]{0:T(1024)S(1)} %bitcast.21, f32[1024]{0:T(1024)S(1)} %bitcast.22, f32[512]{0:T(512)S(1)} %bitcast.26, ...), kind=kOutput, calls=%fused_computation.24 | convolution fusion | flops 819986432 | bytes 2928644 | tf_op jit(solution)/shard_map/while/body/eval_jaxpr/cond/branch_1_fun/dot_general | solution.py:63
  221.0 8.8 %conditional.2 = (f32[512,128]{1,0:T(8,128)S(1)}) conditional(s32[]{:T(128)} %bitcast.16, () %tuple.83, (s32[]{:T(128)}, s32[2048]{0:T(1024)S(1)}, bf16[128,128]{1,0:T(8,128)(2,1)S(1)}, s32[]{:T(128)}, s32[4096]{0:T(1024)}, /*index=5*/f32[3,2048]{1,0:T(4,128)S(1)}, f32[3,4096]{1,0:T(4,128)}, f32[3,2048]{1,0:T(4,128)}, f32[3,4096]{1,0:T(4,128)S(1)}, ...), branch_computations={%region_4.4_spmd, %region_5.5_spmd} | conditional | flops 971244544 | bytes 5163269 | solution.py:137
  222.4 0.9 constant_dynamic-slice_fusion
  224.0 0.9 constant_dynamic-slice_fusion.1
  224.9 4.8 %fusion.14 = f32[512,128]{1,0:T(8,128)S(1)} fusion(f32[512,1024]{1,0:T(8,128)S(1)} %fusion.16, f32[1024]{0:T(1024)S(1)} %get-tuple-element.470, f32[1024]{0:T(1024)S(1)} %get-tuple-element.471, f32[1024]{0:T(1024)S(1)} %bitcast.20, f32[1024]{0:T(1024)S(1)} %bitcast.21, f32[1024]{0:T(1024)S(1)} %bitcast.22, f32[512]{0:T(512)S(1)} %bitcast.26, ...), kind=kOutput, calls=%fused_computation.24 | convolution fusion | flops 819986432 | bytes 2928644 | tf_op jit(solution)/shard_map/while/body/eval_jaxpr/cond/branch_1_fun/dot_general | solution.py:63
  232.4 8.8 %conditional.2 = (f32[512,128]{1,0:T(8,128)S(1)}) conditional(s32[]{:T(128)} %bitcast.16, () %tuple.83, (s32[]{:T(128)}, s32[2048]{0:T(1024)S(1)}, bf16[128,128]{1,0:T(8,128)(2,1)S(1)}, s32[]{:T(128)}, s32[4096]{0:T(1024)}, /*index=5*/f32[3,2048]{1,0:T(4,128)S(1)}, f32[3,4096]{1,0:T(4,128)}, f32[3,2048]{1,0:T(4,128)}, f32[3,4096]{1,0:T(4,128)S(1)}, ...), branch_computations={%region_4.4_spmd, %region_5.5_spmd} | conditional | flops 971244544 | bytes 5163269 | solution.py:137
  233.8 0.9 constant_dynamic-slice_fusion
  235.5 0.9 constant_dynamic-slice_fusion.1
  236.4 4.8 %fusion.14 = f32[512,128]{1,0:T(8,128)S(1)} fusion(f32[512,1024]{1,0:T(8,128)S(1)} %fusion.16, f32[1024]{0:T(1024)S(1)} %get-tuple-element.470, f32[1024]{0:T(1024)S(1)} %get-tuple-element.471, f32[1024]{0:T(1024)S(1)} %bitcast.20, f32[1024]{0:T(1024)S(1)} %bitcast.21, f32[1024]{0:T(1024)S(1)} %bitcast.22, f32[512]{0:T(512)S(1)} %bitcast.26, ...), kind=kOutput, calls=%fused_computation.24 | convolution fusion | flops 819986432 | bytes 2928644 | tf_op jit(solution)/shard_map/while/body/eval_jaxpr/cond/branch_1_fun/dot_general | solution.py:63
  242.5 8.8 %conditional.2 = (f32[512,128]{1,0:T(8,128)S(1)}) conditional(s32[]{:T(128)} %bitcast.16, () %tuple.83, (s32[]{:T(128)}, s32[2048]{0:T(1024)S(1)}, bf16[128,128]{1,0:T(8,128)(2,1)S(1)}, s32[]{:T(128)}, s32[4096]{0:T(1024)}, /*index=5*/f32[3,2048]{1,0:T(4,128)S(1)}, f32[3,4096]{1,0:T(4,128)}, f32[3,2048]{1,0:T(4,128)}, f32[3,4096]{1,0:T(4,128)S(1)}, ...), branch_computations={%region_4.4_spmd, %region_5.5_spmd} | conditional | flops 971244544 | bytes 5163269 | solution.py:137
  243.9 0.9 constant_dynamic-slice_fusion
  245.6 0.9 constant_dynamic-slice_fusion.1
  246.5 4.8 %fusion.14 = f32[512,128]{1,0:T(8,128)S(1)} fusion(f32[512,1024]{1,0:T(8,128)S(1)} %fusion.16, f32[1024]{0:T(1024)S(1)} %get-tuple-element.470, f32[1024]{0:T(1024)S(1)} %get-tuple-element.471, f32[1024]{0:T(1024)S(1)} %bitcast.20, f32[1024]{0:T(1024)S(1)} %bitcast.21, f32[1024]{0:T(1024)S(1)} %bitcast.22, f32[512]{0:T(512)S(1)} %bitcast.26, ...), kind=kOutput, calls=%fused_computation.24 | convolution fusion | flops 819986432 | bytes 2928644 | tf_op jit(solution)/shard_map/while/body/eval_jaxpr/cond/branch_1_fun/dot_general | solution.py:63
  252.6 8.8 %conditional.2 = (f32[512,128]{1,0:T(8,128)S(1)}) conditional(s32[]{:T(128)} %bitcast.16, () %tuple.83, (s32[]{:T(128)}, s32[2048]{0:T(1024)S(1)}, bf16[128,128]{1,0:T(8,128)(2,1)S(1)}, s32[]{:T(128)}, s32[4096]{0:T(1024)}, /*index=5*/f32[3,2048]{1,0:T(4,128)S(1)}, f32[3,4096]{1,0:T(4,128)}, f32[3,2048]{1,0:T(4,128)}, f32[3,4096]{1,0:T(4,128)S(1)}, ...), branch_computations={%region_4.4_spmd, %region_5.5_spmd} | conditional | flops 971244544 | bytes 5163269 | solution.py:137
  254.0 0.9 constant_dynamic-slice_fusion
  255.6 0.9 constant_dynamic-slice_fusion.1
  256.6 4.8 %fusion.14 = f32[512,128]{1,0:T(8,128)S(1)} fusion(f32[512,1024]{1,0:T(8,128)S(1)} %fusion.16, f32[1024]{0:T(1024)S(1)} %get-tuple-element.470, f32[1024]{0:T(1024)S(1)} %get-tuple-element.471, f32[1024]{0:T(1024)S(1)} %bitcast.20, f32[1024]{0:T(1024)S(1)} %bitcast.21, f32[1024]{0:T(1024)S(1)} %bitcast.22, f32[512]{0:T(512)S(1)} %bitcast.26, ...), kind=kOutput, calls=%fused_computation.24 | convolution fusion | flops 819986432 | bytes 2928644 | tf_op jit(solution)/shard_map/while/body/eval_jaxpr/cond/branch_1_fun/dot_general | solution.py:63
  265.4 8.8 %conditional.2 = (f32[512,128]{1,0:T(8,128)S(1)}) conditional(s32[]{:T(128)} %bitcast.16, () %tuple.83, (s32[]{:T(128)}, s32[2048]{0:T(1024)S(1)}, bf16[128,128]{1,0:T(8,128)(2,1)S(1)}, s32[]{:T(128)}, s32[4096]{0:T(1024)}, /*index=5*/f32[3,2048]{1,0:T(4,128)S(1)}, f32[3,4096]{1,0:T(4,128)}, f32[3,2048]{1,0:T(4,128)}, f32[3,4096]{1,0:T(4,128)S(1)}, ...), branch_computations={%region_4.4_spmd, %region_5.5_spmd} | conditional | flops 971244544 | bytes 5163269 | solution.py:137
  266.8 0.9 constant_dynamic-slice_fusion
  268.4 0.9 constant_dynamic-slice_fusion.1
  269.3 4.8 %fusion.14 = f32[512,128]{1,0:T(8,128)S(1)} fusion(f32[512,1024]{1,0:T(8,128)S(1)} %fusion.16, f32[1024]{0:T(1024)S(1)} %get-tuple-element.470, f32[1024]{0:T(1024)S(1)} %get-tuple-element.471, f32[1024]{0:T(1024)S(1)} %bitcast.20, f32[1024]{0:T(1024)S(1)} %bitcast.21, f32[1024]{0:T(1024)S(1)} %bitcast.22, f32[512]{0:T(512)S(1)} %bitcast.26, ...), kind=kOutput, calls=%fused_computation.24 | convolution fusion | flops 819986432 | bytes 2928644 | tf_op jit(solution)/shard_map/while/body/eval_jaxpr/cond/branch_1_fun/dot_general | solution.py:63
  275.5 8.8 %conditional.2 = (f32[512,128]{1,0:T(8,128)S(1)}) conditional(s32[]{:T(128)} %bitcast.16, () %tuple.83, (s32[]{:T(128)}, s32[2048]{0:T(1024)S(1)}, bf16[128,128]{1,0:T(8,128)(2,1)S(1)}, s32[]{:T(128)}, s32[4096]{0:T(1024)}, /*index=5*/f32[3,2048]{1,0:T(4,128)S(1)}, f32[3,4096]{1,0:T(4,128)}, f32[3,2048]{1,0:T(4,128)}, f32[3,4096]{1,0:T(4,128)S(1)}, ...), branch_computations={%region_4.4_spmd, %region_5.5_spmd} | conditional | flops 971244544 | bytes 5163269 | solution.py:137
  276.9 0.9 constant_dynamic-slice_fusion
  278.5 0.9 constant_dynamic-slice_fusion.1
  279.4 4.8 %fusion.14 = f32[512,128]{1,0:T(8,128)S(1)} fusion(f32[512,1024]{1,0:T(8,128)S(1)} %fusion.16, f32[1024]{0:T(1024)S(1)} %get-tuple-element.470, f32[1024]{0:T(1024)S(1)} %get-tuple-element.471, f32[1024]{0:T(1024)S(1)} %bitcast.20, f32[1024]{0:T(1024)S(1)} %bitcast.21, f32[1024]{0:T(1024)S(1)} %bitcast.22, f32[512]{0:T(512)S(1)} %bitcast.26, ...), kind=kOutput, calls=%fused_computation.24 | convolution fusion | flops 819986432 | bytes 2928644 | tf_op jit(solution)/shard_map/while/body/eval_jaxpr/cond/branch_1_fun/dot_general | solution.py:63
  288.2 8.8 %conditional.2 = (f32[512,128]{1,0:T(8,128)S(1)}) conditional(s32[]{:T(128)} %bitcast.16, () %tuple.83, (s32[]{:T(128)}, s32[2048]{0:T(1024)S(1)}, bf16[128,128]{1,0:T(8,128)(2,1)S(1)}, s32[]{:T(128)}, s32[4096]{0:T(1024)}, /*index=5*/f32[3,2048]{1,0:T(4,128)S(1)}, f32[3,4096]{1,0:T(4,128)}, f32[3,2048]{1,0:T(4,128)}, f32[3,4096]{1,0:T(4,128)S(1)}, ...), branch_computations={%region_4.4_spmd, %region_5.5_spmd} | conditional | flops 971244544 | bytes 5163269 | solution.py:137
  289.7 0.9 constant_dynamic-slice_fusion
  292.2 4.8 %fusion.14 = f32[512,128]{1,0:T(8,128)S(1)} fusion(f32[512,1024]{1,0:T(8,128)S(1)} %fusion.16, f32[1024]{0:T(1024)S(1)} %get-tuple-element.470, f32[1024]{0:T(1024)S(1)} %get-tuple-element.471, f32[1024]{0:T(1024)S(1)} %bitcast.20, f32[1024]{0:T(1024)S(1)} %bitcast.21, f32[1024]{0:T(1024)S(1)} %bitcast.22, f32[512]{0:T(512)S(1)} %bitcast.26, ...), kind=kOutput, calls=%fused_computation.24 | convolution fusion | flops 819986432 | bytes 2928644 | tf_op jit(solution)/shard_map/while/body/eval_jaxpr/cond/branch_1_fun/dot_general | solution.py:63
  298.3 8.8 %conditional.2 = (f32[512,128]{1,0:T(8,128)S(1)}) conditional(s32[]{:T(128)} %bitcast.16, () %tuple.83, (s32[]{:T(128)}, s32[2048]{0:T(1024)S(1)}, bf16[128,128]{1,0:T(8,128)(2,1)S(1)}, s32[]{:T(128)}, s32[4096]{0:T(1024)}, /*index=5*/f32[3,2048]{1,0:T(4,128)S(1)}, f32[3,4096]{1,0:T(4,128)}, f32[3,2048]{1,0:T(4,128)}, f32[3,4096]{1,0:T(4,128)S(1)}, ...), branch_computations={%region_4.4_spmd, %region_5.5_spmd} | conditional | flops 971244544 | bytes 5163269 | solution.py:137
  299.8 0.9 constant_dynamic-slice_fusion
  302.3 4.8 %fusion.14 = f32[512,128]{1,0:T(8,128)S(1)} fusion(f32[512,1024]{1,0:T(8,128)S(1)} %fusion.16, f32[1024]{0:T(1024)S(1)} %get-tuple-element.470, f32[1024]{0:T(1024)S(1)} %get-tuple-element.471, f32[1024]{0:T(1024)S(1)} %bitcast.20, f32[1024]{0:T(1024)S(1)} %bitcast.21, f32[1024]{0:T(1024)S(1)} %bitcast.22, f32[512]{0:T(512)S(1)} %bitcast.26, ...), kind=kOutput, calls=%fused_computation.24 | convolution fusion | flops 819986432 | bytes 2928644 | tf_op jit(solution)/shard_map/while/body/eval_jaxpr/cond/branch_1_fun/dot_general | solution.py:63
  307.2 1.0 copy-done
  308.2 139.1 %reduce-scatter.2.cloned.1.call-done = f32[128,128]{1,0:T(8,128)} async-done(((f32[2048,128]{1,0:T(8,128)}), f32[128,128]{1,0:T(8,128)}) %reduce-scatter.2.cloned.1.call-update) | async-done | bytes 65552 | tf_op jit(solution)/shard_map/reduce_scatter | solution.py:144
  447.3 1.5 multiply_add_fusion
  (103 shorter events, 37.6 us)
Async XLA Ops:
  6.5 186.7 %all-reduce.3.cloned.1.call-start = ((), (), s32[]{:S(2)}) async-start(), calls=%async_computation.2 | async-start | bytes 229376 | tf_op jit(solution)/shard_map/psum | solution.py:11
  9.2 438.1 %reduce-scatter.2.cloned.1.call-start = ((), (), s32[]{:S(2)}) async-start(), calls=%async_computation.1 | async-start | bytes 1114112 | tf_op jit(solution)/shard_map/reduce_scatter | solution.py:144
  307.2 1.0 copy-start
Sparse Core Ops, SparseCore 0:
  10.5 182.6 all-reduce.2
  308.3 138.9 reduce-scatter.1
where the time goes:
time: 462 us; the launch traced here: 456 us
  waiting for transfers between devices  320 us (69%)
  matrix products  55.3 us (12%)
  local copies, waits for them, and re-layouts  37.9 us (8%)
  other arithmetic  17.9 us (4%)
  between operations  13.5 us (3%)
  loops' own time  11.5 us (2%)
    psum x1, waiting for transfers between devices, spread(): return lax.psum(block, axis)  180 us
    reduce_scatter x1, waiting for transfers between devices, on_device(): lax.psum_scatter(partial_value, 'col', scatter_dimension=0, tiled=True)  139 us
    dot_general x10, matrix products, unit_term(): jnp.dot(tile, col_rad, precision=lax.Precision.HIGHEST, preferred_element...  47.9 us
    another operation x1, loops' own time, on_device(): lax.fori_loop(0, units_rows * units_cols, visit, jnp.zeros((row_block, ba...  10.7 us
    dynamic_slice x16, local copies, waits for them, and re-layouts, visit(): contrib = lax.cond(live_flags[which], work, skipped)  9.56 us
    slice x10, local copies, waits for them, and re-layouts, view_tile(): along_x = col_pos[0][None, :] - row_pos[0][:, None]  9.38 us
  transfers between devices with their start and end apart: 2, of which 2 were waited for; matrix products, arithmetic and copies ran while one was open for 1% of the time, Pallas kernels for 0%

commit v1 on v0

v1 whole, which is shorter than its diff:
```python
import math

import jax
import jax.numpy as jnp
from jax import lax
from jax.experimental import pallas as pl
from jax.experimental.pallas import tpu as pltpu
from jax.sharding import PartitionSpec as P

F32 = jnp.float32
BF16 = jnp.bfloat16
MESH = pl.DeviceIdType.MESH

ROWS = 2048
COLS = 4096
BANDS = 128
PIECE = 256
TILE = 512
STEPS = COLS // TILE
PIECES = ROWS // PIECE
WIDE = 512
CLOSED = 64.0

SIN = (-1 / 6, 1 / 120, -1 / 5040, 1 / 362880, -1 / 39916800, 1 / 6227020800)
COS = (-1 / 2, 1 / 24, -1 / 720, 1 / 40320, -1 / 3628800, 1 / 479001600, -1 / 87178291200)


def sin_cos(angle):
    turns = jnp.floor(angle * (1 / math.pi) + 0.5)
    rest = (angle - turns * 3.140625) - turns * (math.pi - 3.140625)
    sign = 1.0 - 2.0 * (turns * turns)
    square = rest * rest
    odd = jnp.full_like(angle, SIN[-1])
    for factor in SIN[-2::-1]:
        odd = odd * square + factor
    even = jnp.full_like(angle, COS[-1])
    for factor in COS[-2::-1]:
        even = even * square + factor
    return sign * (rest + rest * (square * odd)), sign * (1.0 + square * even)


def rounded(x):
    return x.astype(BF16).astype(F32)


def pieces(x):
    first = rounded(x)
    rest = x - first
    second = rounded(rest)
    return first, second, rounded(rest - second)


def facets(block):
    place = lax.broadcasted_iota(jnp.int32, block.shape, 0)
    pos = jnp.where(place < 3, block, 0.0)
    sine, cosine = sin_cos(block)
    flat = cosine[4:5]
    normal = jnp.where(
        place == 0,
        cosine[3:4] * flat,
        jnp.where(place == 1, sine[3:4] * flat, jnp.where(place == 2, sine[4:5], 0.0)),
    )
    return place, pos, normal


def stacked(place, *lines):
    out = jnp.zeros(place.shape, F32)
    for index, line in enumerate(lines):
        out = jnp.where(place == index, line, out)
    return out


def kernel(
    table,
    b_hbm,
    visible,
    emission,
    reflect,
    out,
    b_full,
    b_two,
    one_of,
    two_of,
    dist_of,
    lhs,
    row_table,
    acc,
    one_a,
    two_a,
    dist_a,
    one_b,
    two_b,
    dist_b,
    sent,
    came,
    first_half,
    second_half,
    core_came,
    z_sent,
    z_came,
    load_sem,
    spread_send,
    spread_recv,
    ring_send,
    ring_recv,
    core_send,
    core_recv,
    z_send,
    z_recv,
):
    row = lax.axis_index("row")
    col = lax.axis_index("col")
    x = col // 4
    z_hi = col // 2 % 2
    core = col % 2
    y = row // 4
    z_lo = row % 4

    load = pltpu.make_async_copy(b_hbm, b_full, load_sem)
    load.start()

    target = (2 * col + z_lo % 2, y // 2 * 4 + z_lo // 2 * 2 + (1 - y % 2))
    source = ((2 * x + (1 - core)) * 4 + z_hi * 2 + row % 2, row // 2)
    right = (row, (x + 1) % 4 * 4 + col % 4)
    left = (row, (x + 3) % 4 * 4 + col % 4)
    sibling = (row, x * 4 + z_hi * 2 + (1 - core))
    across = (row, x * 4 + (1 - z_hi) * 2 + core)

    barrier = pltpu.get_barrier_semaphore()
    for partner in (source, right, left, sibling, across):
        pl.semaphore_signal(barrier, inc=1, device_id=partner, device_id_type=MESH)
    pl.semaphore_wait(barrier, 5)

    half = pl.multiple_of(z_lo % 2 * ROWS, ROWS)
    spread = pltpu.make_async_remote_copy(
        src_ref=table.at[:, pl.ds(half, ROWS)],
        dst_ref=row_table,
        send_sem=spread_send,
        recv_sem=spread_recv,
        device_id=target,
        device_id_type=MESH,
    )
    spread.start()

    shut = ((visible[...].astype(F32) - 1.0) * CLOSED).astype(BF16)

    def column_tables(step, carry):
        lanes = pl.ds(pl.multiple_of(step * WIDE, WIDE), WIDE)
        block = table[:, lanes]
        place, pos, normal = facets(block)
        alpha = block[5:6] * (1 / math.pi)
        weighted = normal * alpha
        offset = -jnp.sum(weighted * pos, axis=0, keepdims=True)
        reach = jnp.sum(pos * pos, axis=0, keepdims=True) + alpha
        p1, p2, p3 = pieces(pos)
        m1, m2, m3 = pieces(weighted)
        t1, t2, t3 = pieces(offset)
        w1, w2, w3 = pieces(reach)
        zero = jnp.zeros_like(block)
        ones = jnp.where(place < 3, 1.0, zero)
        one_of[0:128, lanes] = jnp.concatenate(
            [p1, p2, p3, p1, p2, p1, ones] + [zero] * 9, axis=0
        ).astype(BF16)
        two_of[:, lanes] = jnp.concatenate(
            [zero] * 7 + [m1, m2, m3, m1, m2, m1, stacked(place, t1, t2, t3), zero, zero], axis=0
        ).astype(BF16)
        d1, d2, d3 = -2.0 * p1, -2.0 * p2, -2.0 * p3
        dist_of[:, lanes] = jnp.concatenate(
            [zero] * 7
            + [d1, d2, d3, d1, d2, d1, stacked(place, w1, w2, w3, 1.0, 1.0, 1.0), zero, zero],
            axis=0,
        ).astype(BF16)
        ids = block[6:7].astype(jnp.int32)
        block_ids = lax.broadcasted_iota(jnp.int32, (128, WIDE), 0)
        onehot = jnp.where(block_ids == ids, 1.0, 0.0).astype(BF16)
        one_of[128:256, lanes] = jnp.dot(shut, onehot, preferred_element_type=F32).astype(BF16)
        return carry

    lax.fori_loop(0, COLS // WIDE, column_tables, 0)

    load.wait()

    def split_radiosity(step, carry):
        rows = pl.ds(pl.multiple_of(step * 256, 256), 256)
        value = b_full[rows, :]
        high = value.astype(BF16)
        b_two[rows, 0:128] = high
        b_two[rows, 128:256] = (value - high.astype(F32)).astype(BF16)
        return carry

    lax.fori_loop(0, COLS // 256, split_radiosity, 0)

    spread.wait_recv()

    def row_tables(step, carry):
        lanes = pl.ds(pl.multiple_of(step * 128, 128), 128)
        block = row_table[:, lanes]
        place, pos, normal = facets(block)
        start = -jnp.sum(normal * pos, axis=0, keepdims=True)
        reach = jnp.sum(pos * pos, axis=0, keepdims=True)
        q1, q2, q3 = pieces(pos)
        n1, n2, n3 = pieces(normal)
        s1, s2, s3 = pieces(start)
        r1, r2, r3 = pieces(reach)
        zero = jnp.zeros_like(block)
        groups = [n1, n1, n1, n2, n2, n3, stacked(place, s1, s2, s3)]
        groups += [q1, q1, q1, q2, q2, q3, stacked(place, 1.0, 1.0, 1.0, r1, r2, r3), zero, zero]
        lhs[lanes, 0:128] = jnp.concatenate(groups, axis=0).T.astype(BF16)
        ids = block[6:7].astype(jnp.int32)
        block_ids = lax.broadcasted_iota(jnp.int32, (128, 128), 0)
        lhs[lanes, 128:256] = jnp.where(block_ids == ids, 1.0, 0.0).T.astype(BF16)
        return carry

    lax.fori_loop(0, ROWS // 128, row_tables, 0)

    def half_of(piece):
        return jnp.where(piece < 6, piece % 2, jnp.where(piece == 6, 1 - z_hi, z_hi))

    def first_row(piece):
        side = half_of(piece)
        hop = piece // 2
        owner = jnp.where(side == 0, x + 3 - hop, x + 1 + hop) % 4
        return pl.multiple_of(owner * 512 + side * PIECE, PIECE)

    slots = ((one_a, two_a, dist_a), (one_b, two_b, dist_b))

    def geometry(begin, tile, slot):
        rows = pl.ds(begin, PIECE)
        lanes = pl.ds(pl.multiple_of(tile * TILE, TILE), TILE)
        slot[0][...] = jnp.dot(lhs[rows, :], one_of[:, lanes], preferred_element_type=F32)
        slot[1][...] = jnp.dot(lhs[rows, 0:128], two_of[:, lanes], preferred_element_type=F32)
        slot[2][...] = jnp.dot(lhs[rows, 0:128], dist_of[:, lanes], preferred_element_type=F32)

    def view(slot):
        for lane in range(0, TILE, 128):
            for line in range(0, PIECE, 16):
                part = (slice(line, line + 16), slice(lane, lane + 128))
                dist = slot[2][part]
                both = jnp.maximum(slot[0][part], 0.0) * jnp.maximum(slot[1][part], 0.0)
                slot[2][part] = both * pl.reciprocal(dist * dist, approx=True)

    def gather(tile, slot):
        value = slot[2][...]
        high = value.astype(BF16)
        low = (value - high.astype(F32)).astype(BF16)
        rad = b_two[pl.ds(pl.multiple_of(tile * TILE, TILE), TILE), :]
        total = jnp.dot(high, rad, preferred_element_type=F32)
        total += jnp.dot(low, rad, preferred_element_type=F32)
        acc[...] += total

    def ring(piece):
        return pltpu.make_async_remote_copy(
            src_ref=sent.at[piece],
            dst_ref=came.at[piece],
            send_sem=ring_send.at[piece],
            recv_sem=ring_recv.at[piece],
            device_id=(row, (x + jnp.where(piece % 2 == 0, 1, 3)) % 4 * 4 + col % 4),
            device_id_type=MESH,
        )

    other_rows = pl.ds(pl.multiple_of((1 - core) * 128, 128), 128)
    own_rows = pl.ds(pl.multiple_of(core * 128, 128), 128)

    def core_copy(index, source_ref):
        return pltpu.make_async_remote_copy(
            src_ref=source_ref.at[other_rows],
            dst_ref=core_came.at[index],
            send_sem=core_send.at[index],
            recv_sem=core_recv.at[index],
            device_id=sibling,
            device_id_type=MESH,
        )

    z_copy = pltpu.make_async_remote_copy(
        src_ref=z_sent,
        dst_ref=z_came,
        send_sem=z_send,
        recv_sem=z_recv,
        device_id=across,
        device_id_type=MESH,
    )

    def folded():
        return acc[:, 0:128] + acc[:, 128:256]

    pairs = STEPS // 2
    acc[...] = jnp.zeros_like(acc)
    geometry(first_row(0), 0, slots[0])

    def visit(index, carry):
        piece = index // pairs
        tile = index % pairs * 2
        begin = first_row(piece)
        after = jnp.minimum(index + 1, PIECES * pairs - 1)
        geometry(begin, tile + 1, slots[1])
        view(slots[0])
        gather(tile, slots[0])
        geometry(first_row(after // pairs), after % pairs * 2, slots[0])
        view(slots[1])
        gather(tile + 1, slots[1])

        @pl.when(tile == STEPS - 2)
        def _():
            @pl.when(piece < 2)
            def _():
                sent[piece] = folded()
                ring(piece).start()

            @pl.when((piece >= 2) & (piece < 6))
            def _():
                ring(piece - 2).wait_recv()
                sent[piece] = folded() + came[piece - 2]
                ring(piece).start()

            @pl.when(piece == 6)
            def _():
                ring(5 - z_hi).wait_recv()
                first_half[...] = folded() + came[5 - z_hi]
                core_copy(0, first_half).start()

            @pl.when(piece < 7)
            def _():
                acc[...] = jnp.zeros_like(acc)

        @pl.when((piece == 7) & (tile == 2))
        def _():
            core_copy(0, first_half).wait_recv()
            z_sent[...] = first_half[own_rows, :] + core_came[0]
            z_copy.start()

        return carry

    lax.fori_loop(0, PIECES * pairs, visit, 0)

    ring(4 + z_hi).wait_recv()
    second_half[...] = folded() + came[4 + z_hi]
    core_copy(1, second_half).start()
    z_copy.wait_recv()
    partial = second_half[own_rows, :] + z_came[...]
    core_copy(1, second_half).wait_recv()
    out[...] = emission[...] + reflect[...] * (partial + core_came[1])

    spread.wait_send()
    for piece in range(6):
        ring(piece).wait_send()
    core_copy(0, first_half).wait_send()
    core_copy(1, second_half).wait_send()
    z_copy.wait_send()


def on_device(b_old, positions, angles, areas, visible, assign, emission, reflect):
    table = jnp.concatenate(
        [
            positions,
            angles,
            areas[None, :],
            assign.astype(F32)[None, :],
            jnp.zeros((1, areas.shape[0]), F32),
        ],
        axis=0,
    )
    vmem = pl.BlockSpec(memory_space=pltpu.VMEM)
    return pl.pallas_call(
        kernel,
        out_shape=jax.ShapeDtypeStruct((128, BANDS), F32),
        in_specs=[vmem, pl.BlockSpec(memory_space=pl.ANY), vmem, vmem, vmem],
        out_specs=vmem,
        scratch_shapes=[
            pltpu.VMEM((COLS, BANDS), F32),
            pltpu.VMEM((COLS, 2 * BANDS), BF16),
            pltpu.VMEM((256, COLS), BF16),
            pltpu.VMEM((128, COLS), BF16),
            pltpu.VMEM((128, COLS), BF16),
            pltpu.VMEM((ROWS, 256), BF16),
            pltpu.VMEM((8, ROWS), F32),
            pltpu.VMEM((PIECE, 2 * BANDS), F32),
        ]
        + [pltpu.VMEM((PIECE, TILE), F32)] * 6
        + [
            pltpu.VMEM((6, PIECE, BANDS), F32),
            pltpu.VMEM((6, PIECE, BANDS), F32),
            pltpu.VMEM((PIECE, BANDS), F32),
            pltpu.VMEM((PIECE, BANDS), F32),
            pltpu.VMEM((2, 128, BANDS), F32),
            pltpu.VMEM((128, BANDS), F32),
            pltpu.VMEM((128, BANDS), F32),
            pltpu.SemaphoreType.DMA,
            pltpu.SemaphoreType.DMA,
            pltpu.SemaphoreType.DMA,
            pltpu.SemaphoreType.DMA((6,)),
            pltpu.SemaphoreType.DMA((6,)),
            pltpu.SemaphoreType.DMA((2,)),
            pltpu.SemaphoreType.DMA((2,)),
            pltpu.SemaphoreType.DMA,
            pltpu.SemaphoreType.DMA,
        ],
        compiler_params=pltpu.CompilerParams(
            collective_id=0, has_side_effects=True, vmem_limit_bytes=48 * 2**20
        ),
        name="radiosity",
    )(table, b_old, visible, emission, reflect)


def solution(mesh):
    return jax.shard_map(
        on_device,
        mesh=mesh,
        in_specs=(
            P("col", None),
            P(None, "col"),
            P(None, "col"),
            P("col"),
            P(),
            P("col"),
            P(("row", "col"), None),
            P(("row", "col"), None),
        ),
        out_specs=P(("row", "col"), None),
        check_vma=False,
    )
```

time: 462 us -> 72.8 us (0.16)
  the two profiles are of different devices: /device:TPU:24 before, /device:TPU:32 now
where the time goes in v1:
time: 72.8 us; the launch traced here: 72.4 us
  Pallas kernels  65.9 us (91%)
  local copies, waits for them, and re-layouts  5.73 us (8%)
    pallas_call x1, Pallas kernels, on_device(): pl.pallas_call(kernel, out_shape=jax.ShapeDtypeStruct((128, BANDS), F32),...  65.9 us
    unnamed x9, local copies, waits for them, and re-layouts  4.74 us

profile of v1, /device:TPU:32, one launch (start us, length us, event | category | flops | bytes accessed | tf_op | source)
XLA Modules:
  0.0 72.4 jit_solution(413264962005398276)
XLA Ops:
  0.0 0.7 convert_element_type.3
  0.7 1.0 %concatenate.3.table = f32[8,4096]{1,0:T(8,128)S(1)} concatenate(f32[3,4096]{1,0:T(4,128)} %param.9, f32[2,4096]{1,0:T(2,128)} %param.10, f32[1,4096]{1,0:T(1,128)} %bitcast.3, f32[1,4096]{1,0:T(1,128)S(1)} %bitcast.2, f32[1,4096]{1,0:T(1,128)S(1)} %broadcast_in_dim.11), dimensions={0} | concatenate | bytes 262144 | tf_op jit(solution)/shard_map/concatenate | solution.py:352
  1.7 0.0 copy-start
  1.7 1.6 %copy-done = f32[4096,128]{1,0:T(8,128)S(1)} copy-done((f32[4096,128]{1,0:T(8,128)S(1)}, f32[4096,128]{1,0:T(8,128)}, u32[]{:S(2)}) %copy-start) | copy-done | bytes 2097176
  3.3 0.0 copy-start.1
  3.3 0.8 %copy-done.1 = s32[128,128]{1,0:T(8,128)S(1)} copy-done((s32[128,128]{1,0:T(8,128)S(1)}, s32[128,128]{1,0:T(8,128)}, u32[]{:S(2)}) %copy-start.1) | copy-done | bytes 65560
  4.2 0.0 copy-start.2
  4.2 0.8 %copy-done.2 = f32[128,128]{1,0:T(8,128)S(1)} copy-done((f32[128,128]{1,0:T(8,128)S(1)}, f32[128,128]{1,0:T(8,128)}, u32[]{:S(2)}) %copy-start.2) | copy-done | bytes 65560
  5.0 0.0 copy-start.3
  5.0 0.8 %copy-done.3 = f32[128,128]{1,0:T(8,128)S(1)} copy-done((f32[128,128]{1,0:T(8,128)S(1)}, f32[128,128]{1,0:T(8,128)}, u32[]{:S(2)}) %copy-start.3) | copy-done | bytes 65560
  5.8 65.9 %radiosity.1 = f32[128,128]{1,0:T(8,128)S(1)} custom-call(f32[8,4096]{1,0:T(8,128)S(1)} %concatenate.3.table, f32[4096,128]{1,0:T(8,128)S(1)} %copy-done, s32[128,128]{1,0:T(8,128)S(1)} %copy-done.1, f32[128,128]{1,0:T(8,128)S(1)} %copy-done.2, f32[128,128]{1,0:T(8,128)S(1)} %copy-done.3), custom_call_target="tpu_custom_call" | custom-call | tf_op jit(solution)/shard_map/radiosity/pallas_call | solution.py:363
  71.8 0.6 copy.10
  (1 shorter events, 0.0 us)
Async XLA Ops:
  1.7 1.6 %copy-start = (f32[4096,128]{1,0:T(8,128)S(1)}, f32[4096,128]{1,0:T(8,128)}, u32[]{:S(2)}) copy-start(f32[4096,128]{1,0:T(8,128)} %b_hbm.1) | copy-start | bytes 6291460
  3.3 0.8 %copy-start.1 = (s32[128,128]{1,0:T(8,128)S(1)}, s32[128,128]{1,0:T(8,128)}, u32[]{:S(2)}) copy-start(s32[128,128]{1,0:T(8,128)} %visible.1) | copy-start | bytes 196612
  4.2 0.8 %copy-start.2 = (f32[128,128]{1,0:T(8,128)S(1)}, f32[128,128]{1,0:T(8,128)}, u32[]{:S(2)}) copy-start(f32[128,128]{1,0:T(8,128)} %emission.1) | copy-start | bytes 196612
  5.0 0.8 %copy-start.3 = (f32[128,128]{1,0:T(8,128)S(1)}, f32[128,128]{1,0:T(8,128)}, u32[]{:S(2)}) copy-start(f32[128,128]{1,0:T(8,128)} %reflect.1) | copy-start | bytes 196612

commit v2 on v1

--- a/solution.py
+++ b/solution.py
@@ -71,13 +71,24 @@
 
 
 def kernel(
+    positions_hbm,
+    angles_hbm,
+    areas_hbm,
+    assign_hbm,
+    b_hbm,
+    visible_hbm,
+    emission_hbm,
+    reflect_hbm,
+    out,
+    positions,
+    angles,
+    areas,
+    assign,
     table,
-    b_hbm,
+    b_full,
     visible,
     emission,
     reflect,
-    out,
-    b_full,
     b_two,
     one_of,
     two_of,
@@ -91,6 +102,8 @@
     one_b,
     two_b,
     dist_b,
+    view_a,
+    view_b,
     sent,
     came,
     first_half,
@@ -116,8 +129,23 @@
     y = row // 4
     z_lo = row % 4
 
-    load = pltpu.make_async_copy(b_hbm, b_full, load_sem)
-    load.start()
+    loads = [
+        pltpu.make_async_copy(source, target, load_sem.at[index])
+        for index, (source, target) in enumerate(
+            (
+                (positions_hbm, positions),
+                (angles_hbm, angles),
+                (areas_hbm, areas),
+                (assign_hbm, assign),
+                (visible_hbm, visible),
+                (b_hbm, b_full),
+                (emission_hbm, emission),
+                (reflect_hbm, reflect),
+            )
+        )
+    ]
+    for load in loads:
+        load.start()
 
     target = (2 * col + z_lo % 2, y // 2 * 4 + z_lo // 2 * 2 + (1 - y % 2))
     source = ((2 * x + (1 - core)) * 4 + z_hi * 2 + row % 2, row // 2)
@@ -129,6 +157,13 @@
     barrier = pltpu.get_barrier_semaphore()
     for partner in (source, right, left, sibling, across):
         pl.semaphore_signal(barrier, inc=1, device_id=partner, device_id_type=MESH)
+    for load in loads[0:4]:
+        load.wait()
+    table[0:3, :] = positions[...]
+    table[3:5, :] = angles[...]
+    table[5:6, :] = areas[...]
+    table[6:7, :] = assign[...].astype(F32)
+    table[7:8, :] = jnp.zeros((1, COLS), F32)
     pl.semaphore_wait(barrier, 5)
 
     half = pl.multiple_of(z_lo % 2 * ROWS, ROWS)
@@ -142,6 +177,7 @@
     )
     spread.start()
 
+    loads[4].wait()
     shut = ((visible[...].astype(F32) - 1.0) * CLOSED).astype(BF16)
 
     def column_tables(step, carry):
@@ -159,15 +195,14 @@
         zero = jnp.zeros_like(block)
         ones = jnp.where(place < 3, 1.0, zero)
         one_of[0:128, lanes] = jnp.concatenate(
-            [p1, p2, p3, p1, p2, p1, ones] + [zero] * 9, axis=0
+            [zero] * 8 + [p1, p2, p3, p1, p2, p1, ones, zero], axis=0
         ).astype(BF16)
         two_of[:, lanes] = jnp.concatenate(
-            [zero] * 7 + [m1, m2, m3, m1, m2, m1, stacked(place, t1, t2, t3), zero, zero], axis=0
+            [m1, m2, m3, m1, m2, m1, stacked(place, t1, t2, t3), zero], axis=0
         ).astype(BF16)
         d1, d2, d3 = -2.0 * p1, -2.0 * p2, -2.0 * p3
         dist_of[:, lanes] = jnp.concatenate(
-            [zero] * 7
-            + [d1, d2, d3, d1, d2, d1, stacked(place, w1, w2, w3, 1.0, 1.0, 1.0), zero, zero],
+            [d1, d2, d3, d1, d2, d1, stacked(place, w1, w2, w3, 1.0, 1.0, 1.0), zero],
             axis=0,
         ).astype(BF16)
         ids = block[6:7].astype(jnp.int32)
@@ -178,7 +213,7 @@
 
     lax.fori_loop(0, COLS // WIDE, column_tables, 0)
 
-    load.wait()
+    loads[5].wait()
 
     def split_radiosity(step, carry):
         rows = pl.ds(pl.multiple_of(step * 256, 256), 256)
@@ -203,8 +238,8 @@
         s1, s2, s3 = pieces(start)
         r1, r2, r3 = pieces(reach)
         zero = jnp.zeros_like(block)
-        groups = [n1, n1, n1, n2, n2, n3, stacked(place, s1, s2, s3)]
-        groups += [q1, q1, q1, q2, q2, q3, stacked(place, 1.0, 1.0, 1.0, r1, r2, r3), zero, zero]
+        groups = [q1, q1, q1, q2, q2, q3, stacked(place, 1.0, 1.0, 1.0, r1, r2, r3), zero]
+        groups += [n1, n1, n1, n2, n2, n3, stacked(place, s1, s2, s3), zero]
         lhs[lanes, 0:128] = jnp.concatenate(groups, axis=0).T.astype(BF16)
         ids = block[6:7].astype(jnp.int32)
         block_ids = lax.broadcasted_iota(jnp.int32, (128, 128), 0)
@@ -228,19 +263,19 @@
         rows = pl.ds(begin, PIECE)
         lanes = pl.ds(pl.multiple_of(tile * TILE, TILE), TILE)
         slot[0][...] = jnp.dot(lhs[rows, :], one_of[:, lanes], preferred_element_type=F32)
-        slot[1][...] = jnp.dot(lhs[rows, 0:128], two_of[:, lanes], preferred_element_type=F32)
-        slot[2][...] = jnp.dot(lhs[rows, 0:128], dist_of[:, lanes], preferred_element_type=F32)
-
-    def view(slot):
+        slot[1][...] = jnp.dot(lhs[rows, 0:64], two_of[:, lanes], preferred_element_type=F32)
+        slot[2][...] = jnp.dot(lhs[rows, 0:64], dist_of[:, lanes], preferred_element_type=F32)
+
+    def view(slot, views):
         for lane in range(0, TILE, 128):
             for line in range(0, PIECE, 16):
                 part = (slice(line, line + 16), slice(lane, lane + 128))
                 dist = slot[2][part]
                 both = jnp.maximum(slot[0][part], 0.0) * jnp.maximum(slot[1][part], 0.0)
-                slot[2][part] = both * pl.reciprocal(dist * dist, approx=True)
-
-    def gather(tile, slot):
-        value = slot[2][...]
+                views[part] = both * pl.reciprocal(dist * dist, approx=True)
+
+    def gather(tile, views):
+        value = views[...]
         high = value.astype(BF16)
         low = (value - high.astype(F32)).astype(BF16)
         rad = b_two[pl.ds(pl.multiple_of(tile * TILE, TILE), TILE), :]
@@ -284,20 +319,26 @@
         return acc[:, 0:128] + acc[:, 128:256]
 
     pairs = STEPS // 2
+    tiles = PIECES * STEPS
     acc[...] = jnp.zeros_like(acc)
-    geometry(first_row(0), 0, slots[0])
+
+    def geometry_of(index, slot):
+        geometry(first_row(index // STEPS), index % STEPS, slot)
+
+    geometry_of(0, slots[0])
+    view(slots[0], view_a)
+    geometry_of(1, slots[1])
 
     def visit(index, carry):
         piece = index // pairs
         tile = index % pairs * 2
-        begin = first_row(piece)
-        after = jnp.minimum(index + 1, PIECES * pairs - 1)
-        geometry(begin, tile + 1, slots[1])
-        view(slots[0])
-        gather(tile, slots[0])
-        geometry(first_row(after // pairs), after % pairs * 2, slots[0])
-        view(slots[1])
-        gather(tile + 1, slots[1])
+        after = jnp.minimum(index * 2 + 2, tiles - 2)
+        geometry_of(after, slots[0])
+        view(slots[1], view_b)
+        gather(tile, view_a)
+        geometry_of(after + 1, slots[1])
+        view(slots[0], view_a)
+        gather(tile + 1, view_b)
 
         @pl.when(tile == STEPS - 2)
         def _():
@@ -338,6 +379,8 @@
     z_copy.wait_recv()
     partial = second_half[own_rows, :] + z_came[...]
     core_copy(1, second_half).wait_recv()
+    loads[6].wait()
+    loads[7].wait()
     out[...] = emission[...] + reflect[...] * (partial + core_came[1])
 
     spread.wait_send()
@@ -349,33 +392,31 @@
 
 
 def on_device(b_old, positions, angles, areas, visible, assign, emission, reflect):
-    table = jnp.concatenate(
-        [
-            positions,
-            angles,
-            areas[None, :],
-            assign.astype(F32)[None, :],
-            jnp.zeros((1, areas.shape[0]), F32),
-        ],
-        axis=0,
-    )
     vmem = pl.BlockSpec(memory_space=pltpu.VMEM)
     return pl.pallas_call(
         kernel,
         out_shape=jax.ShapeDtypeStruct((128, BANDS), F32),
-        in_specs=[vmem, pl.BlockSpec(memory_space=pl.ANY), vmem, vmem, vmem],
+        in_specs=[pl.BlockSpec(memory_space=pl.ANY)] * 8,
         out_specs=vmem,
         scratch_shapes=[
+            pltpu.VMEM((3, COLS), F32),
+            pltpu.VMEM((2, COLS), F32),
+            pltpu.VMEM((1, COLS), F32),
+            pltpu.VMEM((1, COLS), jnp.int32),
+            pltpu.VMEM((8, COLS), F32),
             pltpu.VMEM((COLS, BANDS), F32),
+            pltpu.VMEM((128, 128), jnp.int32),
+            pltpu.VMEM((128, BANDS), F32),
+            pltpu.VMEM((128, BANDS), F32),
             pltpu.VMEM((COLS, 2 * BANDS), BF16),
             pltpu.VMEM((256, COLS), BF16),
-            pltpu.VMEM((128, COLS), BF16),
-            pltpu.VMEM((128, COLS), BF16),
+            pltpu.VMEM((64, COLS), BF16),
+            pltpu.VMEM((64, COLS), BF16),
             pltpu.VMEM((ROWS, 256), BF16),
             pltpu.VMEM((8, ROWS), F32),
             pltpu.VMEM((PIECE, 2 * BANDS), F32),
         ]
-        + [pltpu.VMEM((PIECE, TILE), F32)] * 6
+        + [pltpu.VMEM((PIECE, TILE), F32)] * 8
         + [
             pltpu.VMEM((6, PIECE, BANDS), F32),
             pltpu.VMEM((6, PIECE, BANDS), F32),
@@ -384,7 +425,7 @@
             pltpu.VMEM((2, 128, BANDS), F32),
             pltpu.VMEM((128, BANDS), F32),
             pltpu.VMEM((128, BANDS), F32),
-            pltpu.SemaphoreType.DMA,
+            pltpu.SemaphoreType.DMA((8,)),
             pltpu.SemaphoreType.DMA,
             pltpu.SemaphoreType.DMA,
             pltpu.SemaphoreType.DMA((6,)),
@@ -395,10 +436,19 @@
             pltpu.SemaphoreType.DMA,
         ],
         compiler_params=pltpu.CompilerParams(
-            collective_id=0, has_side_effects=True, vmem_limit_bytes=48 * 2**20
+            collective_id=0, has_side_effects=True, vmem_limit_bytes=60 * 2**20
         ),
         name="radiosity",
-    )(table, b_old, visible, emission, reflect)
+    )(
+        positions,
+        angles,
+        areas[None, :],
+        assign[None, :],
+        b_old,
+        visible,
+        emission,
+        reflect,
+    )
 
 
 def solution(mesh):

time: 72.8 us -> 67.7 us (0.930)
  local copies, waits for them, and re-layouts: 5.73 us -> 1.47 us
    unnamed x9 -> x1, local copies, waits for them, and re-layouts: 4.74 us -> 1.47 us
    concatenate x1 -> x0, local copies, waits for them, and re-layouts: 0.98 us -> none  [on_device(): jnp.concatenate([positions, angles, areas[None, :], assign.astype(F32)[No...]
where the time goes in v2:
time: 67.7 us; the launch traced here: 67.5 us
  Pallas kernels  66 us (97%)
  local copies, waits for them, and re-layouts  1.47 us (2%)
    pallas_call x1, Pallas kernels, on_device(): pl.pallas_call(kernel, out_shape=jax.ShapeDtypeStruct((128, BANDS), F32),...  66 us
    unnamed x1, local copies, waits for them, and re-layouts  1.47 us

profile of v2, /device:TPU:32, one launch (start us, length us, event | category | flops | bytes accessed | tf_op | source)
XLA Modules:
  0.0 67.5 jit_solution(9555601509734449570)
XLA Ops:
  0.0 66.0 %radiosity.1 = f32[128,128]{1,0:T(8,128)} custom-call(f32[3,4096]{1,0:T(4,128)} %positions_hbm.1, f32[2,4096]{1,0:T(2,128)} %angles_hbm.1, f32[1,4096]{1,0:T(1,128)} %bitcast.2, s32[1,4096]{1,0:T(1,128)} %bitcast.3, f32[4096,128]{1,0:T(8,128)} %b_hbm.1, s32[128,128]{1,0:T(8,128)} %visible_hbm.1, f32[128,128]{1,0:T(8,128)} %emission_hbm.1, f32[128,128]{1,0:T(8,128)} %reflect_hbm.1), custom_call_target="tpu_custom_call" | custom-call | tf_op jit(solution)/shard_map/radiosity/pallas_call | solution.py:396
  66.0 1.5 %copy.10 = f32[128,128]{1,0:T(8,128)} copy(f32[128,128]{1,0:T(8,128)} %radiosity.1) | data formatting | bytes 131072

commit v3 on v2

--- a/solution.py
+++ b/solution.py
@@ -113,6 +113,7 @@
     z_came,
     load_sem,
     spread_send,
+    forward_send,
     spread_recv,
     ring_send,
     ring_recv,
@@ -126,8 +127,9 @@
     x = col // 4
     z_hi = col // 2 % 2
     core = col % 2
-    y = row // 4
-    z_lo = row % 4
+    is_source = col == row // 2
+    serves = core == row // 2 % 2
+    is_leader = serves & jnp.logical_not(is_source)
 
     loads = [
         pltpu.make_async_copy(source, target, load_sem.at[index])
@@ -147,16 +149,19 @@
     for load in loads:
         load.start()
 
-    target = (2 * col + z_lo % 2, y // 2 * 4 + z_lo // 2 * 2 + (1 - y % 2))
-    source = ((2 * x + (1 - core)) * 4 + z_hi * 2 + row % 2, row // 2)
     right = (row, (x + 1) % 4 * 4 + col % 4)
     left = (row, (x + 3) % 4 * 4 + col % 4)
     sibling = (row, x * 4 + z_hi * 2 + (1 - core))
     across = (row, x * 4 + (1 - z_hi) * 2 + core)
 
     barrier = pltpu.get_barrier_semaphore()
-    for partner in (source, right, left, sibling, across):
+    for partner in (right, left, sibling, across):
         pl.semaphore_signal(barrier, inc=1, device_id=partner, device_id_type=MESH)
+
+    @pl.when(is_leader)
+    def _():
+        pl.semaphore_signal(barrier, inc=1, device_id=(row, row // 2), device_id_type=MESH)
+
     for load in loads[0:4]:
         load.wait()
     table[0:3, :] = positions[...]
@@ -164,18 +169,33 @@
     table[5:6, :] = areas[...]
     table[6:7, :] = assign[...].astype(F32)
     table[7:8, :] = jnp.zeros((1, COLS), F32)
-    pl.semaphore_wait(barrier, 5)
-
-    half = pl.multiple_of(z_lo % 2 * ROWS, ROWS)
-    spread = pltpu.make_async_remote_copy(
-        src_ref=table.at[:, pl.ds(half, ROWS)],
+    pl.semaphore_wait(barrier, jnp.where(is_source, 11, 4))
+
+    def spread(hop):
+        return pltpu.make_async_remote_copy(
+            src_ref=table.at[:, pl.ds(pl.multiple_of(row % 2 * ROWS, ROWS), ROWS)],
+            dst_ref=row_table,
+            send_sem=spread_send.at[hop - 1],
+            recv_sem=spread_recv,
+            device_id=(row, (row // 4 + hop) % 8 * 2 + core),
+            device_id_type=MESH,
+        )
+
+    forward = pltpu.make_async_remote_copy(
+        src_ref=row_table,
         dst_ref=row_table,
-        send_sem=spread_send,
+        send_sem=forward_send,
         recv_sem=spread_recv,
-        device_id=target,
+        device_id=sibling,
         device_id_type=MESH,
     )
-    spread.start()
+
+    @pl.when(is_source)
+    def _():
+        for hop in (4, 3, 5, 2, 6, 1, 7):
+            spread(hop).start()
+        row_table[...] = table[:, pl.ds(pl.multiple_of(row % 2 * ROWS, ROWS), ROWS)]
+        forward.start()
 
     loads[4].wait()
     shut = ((visible[...].astype(F32) - 1.0) * CLOSED).astype(BF16)
@@ -213,6 +233,11 @@
 
     lax.fori_loop(0, COLS // WIDE, column_tables, 0)
 
+    @pl.when(is_leader)
+    def _():
+        spread(1).wait_recv()
+        forward.start()
+
     loads[5].wait()
 
     def split_radiosity(step, carry):
@@ -225,7 +250,10 @@
 
     lax.fori_loop(0, COLS // 256, split_radiosity, 0)
 
-    spread.wait_recv()
+    @pl.when(jnp.logical_not(serves))
+    def _():
+        forward.wait_recv()
+
 
     def row_tables(step, carry):
         lanes = pl.ds(pl.multiple_of(step * 128, 128), 128)
@@ -383,7 +411,15 @@
     loads[7].wait()
     out[...] = emission[...] + reflect[...] * (partial + core_came[1])
 
-    spread.wait_send()
+    @pl.when(is_source)
+    def _():
+        for hop in range(1, 8):
+            spread(hop).wait_send()
+
+    @pl.when(serves)
+    def _():
+        forward.wait_send()
+
     for piece in range(6):
         ring(piece).wait_send()
     core_copy(0, first_half).wait_send()
@@ -426,6 +462,7 @@
             pltpu.VMEM((128, BANDS), F32),
             pltpu.VMEM((128, BANDS), F32),
             pltpu.SemaphoreType.DMA((8,)),
+            pltpu.SemaphoreType.DMA((7,)),
             pltpu.SemaphoreType.DMA,
             pltpu.SemaphoreType.DMA,
             pltpu.SemaphoreType.DMA((6,)),

time: 67.7 us -> 59.7 us (0.88)
  the two profiles are of different devices: /device:TPU:32 before, /device:TPU:81 now
where the time goes in v3:
time: 59.7 us; the launch traced here: 59.5 us
  Pallas kernels  58 us (97%)
  local copies, waits for them, and re-layouts  1.47 us (2%)
    pallas_call x1, Pallas kernels, on_device(): pl.pallas_call(kernel, out_shape=jax.ShapeDtypeStruct((128, BANDS), F32),...  58 us
    unnamed x1, local copies, waits for them, and re-layouts  1.47 us

profile of v3, /device:TPU:81, one launch (start us, length us, event | category | flops | bytes accessed | tf_op | source)
XLA Modules:
  0.0 59.5 jit_solution(8930826566002945456)
XLA Ops:
  0.0 58.0 %radiosity.1 = f32[128,128]{1,0:T(8,128)} custom-call(f32[3,4096]{1,0:T(4,128)} %positions_hbm.1, f32[2,4096]{1,0:T(2,128)} %angles_hbm.1, f32[1,4096]{1,0:T(1,128)} %bitcast.2, s32[1,4096]{1,0:T(1,128)} %bitcast.3, f32[4096,128]{1,0:T(8,128)} %b_hbm.1, s32[128,128]{1,0:T(8,128)} %visible_hbm.1, f32[128,128]{1,0:T(8,128)} %emission_hbm.1, f32[128,128]{1,0:T(8,128)} %reflect_hbm.1), custom_call_target="tpu_custom_call" | custom-call | tf_op jit(solution)/shard_map/radiosity/pallas_call | solution.py:432
  58.1 1.5 %copy.10 = f32[128,128]{1,0:T(8,128)} copy(f32[128,128]{1,0:T(8,128)} %radiosity.1) | data formatting | bytes 131072

commit v4 on v3

--- a/solution.py
+++ b/solution.py
@@ -113,6 +113,7 @@
     z_came,
     load_sem,
     spread_send,
+    over_send,
     forward_send,
     spread_recv,
     ring_send,
@@ -127,9 +128,12 @@
     x = col // 4
     z_hi = col // 2 % 2
     core = col % 2
-    is_source = col == row // 2
-    serves = core == row // 2 % 2
-    is_leader = serves & jnp.logical_not(is_source)
+    home = row // 2
+    serves = core == home % 2
+    near = serves & (z_hi == home // 2 % 2)
+    is_source = col == home
+    is_relay = near & jnp.logical_not(is_source)
+    is_far = serves & jnp.logical_not(near)
 
     loads = [
         pltpu.make_async_copy(source, target, load_sem.at[index])
@@ -158,9 +162,9 @@
     for partner in (right, left, sibling, across):
         pl.semaphore_signal(barrier, inc=1, device_id=partner, device_id_type=MESH)
 
-    @pl.when(is_leader)
-    def _():
-        pl.semaphore_signal(barrier, inc=1, device_id=(row, row // 2), device_id_type=MESH)
+    @pl.when(near & (x == (home // 4 + 2) % 4))
+    def _():
+        pl.semaphore_signal(barrier, inc=1, device_id=(row, home), device_id_type=MESH)
 
     for load in loads[0:4]:
         load.wait()
@@ -169,7 +173,7 @@
     table[5:6, :] = areas[...]
     table[6:7, :] = assign[...].astype(F32)
     table[7:8, :] = jnp.zeros((1, COLS), F32)
-    pl.semaphore_wait(barrier, jnp.where(is_source, 11, 4))
+    pl.semaphore_wait(barrier, jnp.where(is_source, 5, 4))
 
     def spread(hop):
         return pltpu.make_async_remote_copy(
@@ -177,7 +181,7 @@
             dst_ref=row_table,
             send_sem=spread_send.at[hop - 1],
             recv_sem=spread_recv,
-            device_id=(row, (row // 4 + hop) % 8 * 2 + core),
+            device_id=(row, (x + hop) % 4 * 4 + col % 4),
             device_id_type=MESH,
         )
 
@@ -190,11 +194,21 @@
         device_id_type=MESH,
     )
 
+    over = pltpu.make_async_remote_copy(
+        src_ref=row_table,
+        dst_ref=row_table,
+        send_sem=over_send,
+        recv_sem=spread_recv,
+        device_id=across,
+        device_id_type=MESH,
+    )
+
     @pl.when(is_source)
     def _():
-        for hop in (4, 3, 5, 2, 6, 1, 7):
+        for hop in (2, 1, 3):
             spread(hop).start()
         row_table[...] = table[:, pl.ds(pl.multiple_of(row % 2 * ROWS, ROWS), ROWS)]
+        over.start()
         forward.start()
 
     loads[4].wait()
@@ -233,9 +247,10 @@
 
     lax.fori_loop(0, COLS // WIDE, column_tables, 0)
 
-    @pl.when(is_leader)
+    @pl.when(is_relay)
     def _():
         spread(1).wait_recv()
+        over.start()
         forward.start()
 
     loads[5].wait()
@@ -250,13 +265,18 @@
 
     lax.fori_loop(0, COLS // 256, split_radiosity, 0)
 
+    @pl.when(is_far)
+    def _():
+        over.wait_recv()
+        forward.start()
+
     @pl.when(jnp.logical_not(serves))
     def _():
         forward.wait_recv()
 
 
     def row_tables(step, carry):
-        lanes = pl.ds(pl.multiple_of(step * 128, 128), 128)
+        lanes = pl.ds(pl.multiple_of(step * 256, 256), 256)
         block = row_table[:, lanes]
         place, pos, normal = facets(block)
         start = -jnp.sum(normal * pos, axis=0, keepdims=True)
@@ -270,18 +290,23 @@
         groups += [n1, n1, n1, n2, n2, n3, stacked(place, s1, s2, s3), zero]
         lhs[lanes, 0:128] = jnp.concatenate(groups, axis=0).T.astype(BF16)
         ids = block[6:7].astype(jnp.int32)
-        block_ids = lax.broadcasted_iota(jnp.int32, (128, 128), 0)
+        block_ids = lax.broadcasted_iota(jnp.int32, (128, 256), 0)
         lhs[lanes, 128:256] = jnp.where(block_ids == ids, 1.0, 0.0).T.astype(BF16)
         return carry
 
-    lax.fori_loop(0, ROWS // 128, row_tables, 0)
+    lax.fori_loop(0, ROWS // 256, row_tables, 0)
+
+    def hop_of(piece):
+        between = jnp.where(piece % 2 == 1, (piece + 1) // 2, piece // 2 - 1)
+        return jnp.where(piece == 0, 0, jnp.where(piece == 7, 3, between))
 
     def half_of(piece):
-        return jnp.where(piece < 6, piece % 2, jnp.where(piece == 6, 1 - z_hi, z_hi))
+        stays = (piece == 7) | ((piece > 0) & (piece % 2 == 0))
+        return jnp.where(stays, z_hi, 1 - z_hi)
 
     def first_row(piece):
         side = half_of(piece)
-        hop = piece // 2
+        hop = hop_of(piece)
         owner = jnp.where(side == 0, x + 3 - hop, x + 1 + hop) % 4
         return pl.multiple_of(owner * 512 + side * PIECE, PIECE)
 
@@ -370,18 +395,21 @@
 
         @pl.when(tile == STEPS - 2)
         def _():
-            @pl.when(piece < 2)
+            hop = hop_of(piece)
+            place = hop * 2 + half_of(piece)
+
+            @pl.when(hop == 0)
             def _():
-                sent[piece] = folded()
-                ring(piece).start()
-
-            @pl.when((piece >= 2) & (piece < 6))
+                sent[place] = folded()
+                ring(place).start()
+
+            @pl.when((hop == 1) | (hop == 2))
             def _():
-                ring(piece - 2).wait_recv()
-                sent[piece] = folded() + came[piece - 2]
-                ring(piece).start()
-
-            @pl.when(piece == 6)
+                ring(place - 2).wait_recv()
+                sent[place] = folded() + came[place - 2]
+                ring(place).start()
+
+            @pl.when(piece == 5)
             def _():
                 ring(5 - z_hi).wait_recv()
                 first_half[...] = folded() + came[5 - z_hi]
@@ -391,7 +419,7 @@
             def _():
                 acc[...] = jnp.zeros_like(acc)
 
-        @pl.when((piece == 7) & (tile == 2))
+        @pl.when((piece == 6) & (tile == 2))
         def _():
             core_copy(0, first_half).wait_recv()
             z_sent[...] = first_half[own_rows, :] + core_came[0]
@@ -413,8 +441,12 @@
 
     @pl.when(is_source)
     def _():
-        for hop in range(1, 8):
+        for hop in range(1, 4):
             spread(hop).wait_send()
+
+    @pl.when(near)
+    def _():
+        over.wait_send()
 
     @pl.when(serves)
     def _():
@@ -462,7 +494,8 @@
             pltpu.VMEM((128, BANDS), F32),
             pltpu.VMEM((128, BANDS), F32),
             pltpu.SemaphoreType.DMA((8,)),
-            pltpu.SemaphoreType.DMA((7,)),
+            pltpu.SemaphoreType.DMA((3,)),
+            pltpu.SemaphoreType.DMA,
             pltpu.SemaphoreType.DMA,
             pltpu.SemaphoreType.DMA,
             pltpu.SemaphoreType.DMA((6,)),

time: 59.7 us -> 56.8 us (0.951)
  the two profiles are of different devices: /device:TPU:81 before, /device:TPU:25 now
where the time goes in v4:
time: 56.8 us; the launch traced here: 56.6 us
  Pallas kernels  55.1 us (97%)
  local copies, waits for them, and re-layouts  1.47 us (3%)
    pallas_call x1, Pallas kernels, on_device(): pl.pallas_call(kernel, out_shape=jax.ShapeDtypeStruct((128, BANDS), F32),...  55.1 us
    unnamed x1, local copies, waits for them, and re-layouts  1.47 us

profile of v4, /device:TPU:25, one launch (start us, length us, event | category | flops | bytes accessed | tf_op | source)
XLA Modules:
  0.0 56.6 jit_solution(12046972221122316993)
XLA Ops:
  0.0 55.1 %radiosity.1 = f32[128,128]{1,0:T(8,128)} custom-call(f32[3,4096]{1,0:T(4,128)} %positions_hbm.1, f32[2,4096]{1,0:T(2,128)} %angles_hbm.1, f32[1,4096]{1,0:T(1,128)} %bitcast.2, s32[1,4096]{1,0:T(1,128)} %bitcast.3, f32[4096,128]{1,0:T(8,128)} %b_hbm.1, s32[128,128]{1,0:T(8,128)} %visible_hbm.1, f32[128,128]{1,0:T(8,128)} %emission_hbm.1, f32[128,128]{1,0:T(8,128)} %reflect_hbm.1), custom_call_target="tpu_custom_call" | custom-call | tf_op jit(solution)/shard_map/radiosity/pallas_call | solution.py:464
  55.2 1.5 %copy.10 = f32[128,128]{1,0:T(8,128)} copy(f32[128,128]{1,0:T(8,128)} %radiosity.1) | data formatting | bytes 131072

commit v5 on v4

--- a/solution.py
+++ b/solution.py
@@ -15,9 +15,11 @@
 COLS = 4096
 BANDS = 128
 PIECE = 256
-TILE = 512
+TILE = 1024
 STEPS = COLS // TILE
 PIECES = ROWS // PIECE
+PARTS = 4
+PART = ROWS // PARTS
 WIDE = 512
 CLOSED = 64.0
 
@@ -175,41 +177,48 @@
     table[7:8, :] = jnp.zeros((1, COLS), F32)
     pl.semaphore_wait(barrier, jnp.where(is_source, 5, 4))
 
-    def spread(hop):
+    def lanes_of(part):
+        return pl.ds(part * PART, PART)
+
+    def spread(hop, part):
         return pltpu.make_async_remote_copy(
-            src_ref=table.at[:, pl.ds(pl.multiple_of(row % 2 * ROWS, ROWS), ROWS)],
-            dst_ref=row_table,
-            send_sem=spread_send.at[hop - 1],
-            recv_sem=spread_recv,
+            src_ref=table.at[:, pl.ds(pl.multiple_of(row % 2 * ROWS + part * PART, PART), PART)],
+            dst_ref=row_table.at[:, lanes_of(part)],
+            send_sem=spread_send.at[(hop - 1) * PARTS + part],
+            recv_sem=spread_recv.at[part],
             device_id=(row, (x + hop) % 4 * 4 + col % 4),
             device_id_type=MESH,
         )
 
-    forward = pltpu.make_async_remote_copy(
-        src_ref=row_table,
-        dst_ref=row_table,
-        send_sem=forward_send,
-        recv_sem=spread_recv,
-        device_id=sibling,
-        device_id_type=MESH,
-    )
-
-    over = pltpu.make_async_remote_copy(
-        src_ref=row_table,
-        dst_ref=row_table,
-        send_sem=over_send,
-        recv_sem=spread_recv,
-        device_id=across,
-        device_id_type=MESH,
-    )
+    def forward(part):
+        return pltpu.make_async_remote_copy(
+            src_ref=row_table.at[:, lanes_of(part)],
+            dst_ref=row_table.at[:, lanes_of(part)],
+            send_sem=forward_send.at[part],
+            recv_sem=spread_recv.at[part],
+            device_id=sibling,
+            device_id_type=MESH,
+        )
+
+    def over(part):
+        return pltpu.make_async_remote_copy(
+            src_ref=row_table.at[:, lanes_of(part)],
+            dst_ref=row_table.at[:, lanes_of(part)],
+            send_sem=over_send.at[part],
+            recv_sem=spread_recv.at[part],
+            device_id=across,
+            device_id_type=MESH,
+        )
 
     @pl.when(is_source)
     def _():
-        for hop in (2, 1, 3):
-            spread(hop).start()
+        for part in range(PARTS):
+            for hop in (2, 1, 3):
+                spread(hop, part).start()
         row_table[...] = table[:, pl.ds(pl.multiple_of(row % 2 * ROWS, ROWS), ROWS)]
-        over.start()
-        forward.start()
+        for part in range(PARTS):
+            over(part).start()
+            forward(part).start()
 
     loads[4].wait()
     shut = ((visible[...].astype(F32) - 1.0) * CLOSED).astype(BF16)
@@ -249,9 +258,10 @@
 
     @pl.when(is_relay)
     def _():
-        spread(1).wait_recv()
-        over.start()
-        forward.start()
+        for part in range(PARTS):
+            spread(1, part).wait_recv()
+            over(part).start()
+            forward(part).start()
 
     loads[5].wait()
 
@@ -267,12 +277,13 @@
 
     @pl.when(is_far)
     def _():
-        over.wait_recv()
-        forward.start()
+        for part in range(PARTS):
+            over(part).wait_recv()
+            forward(part).start()
 
     @pl.when(jnp.logical_not(serves))
     def _():
-        forward.wait_recv()
+        forward(0).wait_recv()
 
 
     def row_tables(step, carry):
@@ -294,7 +305,15 @@
         lhs[lanes, 128:256] = jnp.where(block_ids == ids, 1.0, 0.0).T.astype(BF16)
         return carry
 
-    lax.fori_loop(0, ROWS // 256, row_tables, 0)
+    per_part = PART // 256
+    lax.fori_loop(0, per_part, row_tables, 0)
+    for part in range(1, PARTS):
+
+        @pl.when(jnp.logical_not(serves))
+        def _(part=part):
+            forward(part).wait_recv()
+
+        lax.fori_loop(part * per_part, (part + 1) * per_part, row_tables, 0)
 
     def hop_of(piece):
         between = jnp.where(piece % 2 == 1, (piece + 1) // 2, piece // 2 - 1)
@@ -419,7 +438,7 @@
             def _():
                 acc[...] = jnp.zeros_like(acc)
 
-        @pl.when((piece == 6) & (tile == 2))
+        @pl.when((piece == 6) & (tile == 0))
         def _():
             core_copy(0, first_half).wait_recv()
             z_sent[...] = first_half[own_rows, :] + core_came[0]
@@ -442,15 +461,18 @@
     @pl.when(is_source)
     def _():
         for hop in range(1, 4):
-            spread(hop).wait_send()
+            for part in range(PARTS):
+                spread(hop, part).wait_send()
 
     @pl.when(near)
     def _():
-        over.wait_send()
+        for part in range(PARTS):
+            over(part).wait_send()
 
     @pl.when(serves)
     def _():
-        forward.wait_send()
+        for part in range(PARTS):
+            forward(part).wait_send()
 
     for piece in range(6):
         ring(piece).wait_send()
@@ -494,10 +516,10 @@
             pltpu.VMEM((128, BANDS), F32),
             pltpu.VMEM((128, BANDS), F32),
             pltpu.SemaphoreType.DMA((8,)),
-            pltpu.SemaphoreType.DMA((3,)),
-            pltpu.SemaphoreType.DMA,
-            pltpu.SemaphoreType.DMA,
-            pltpu.SemaphoreType.DMA,
+            pltpu.SemaphoreType.DMA((3 * PARTS,)),
+            pltpu.SemaphoreType.DMA((PARTS,)),
+            pltpu.SemaphoreType.DMA((PARTS,)),
+            pltpu.SemaphoreType.DMA((PARTS,)),
             pltpu.SemaphoreType.DMA((6,)),
             pltpu.SemaphoreType.DMA((6,)),
             pltpu.SemaphoreType.DMA((2,)),

time: 56.8 us -> 54.9 us (0.967)
  the two profiles are of different devices: /device:TPU:25 before, /device:TPU:41 now
where the time goes in v5:
time: 54.9 us; the launch traced here: 54.7 us
  Pallas kernels  53.2 us (97%)
  local copies, waits for them, and re-layouts  1.47 us (3%)
    pallas_call x1, Pallas kernels, on_device(): pl.pallas_call(kernel, out_shape=jax.ShapeDtypeStruct((128, BANDS), F32),...  53.2 us
    unnamed x1, local copies, waits for them, and re-layouts  1.47 us

profile of v5, /device:TPU:41, one launch (start us, length us, event | category | flops | bytes accessed | tf_op | source)
XLA Modules:
  0.0 54.7 jit_solution(6024697132075561622)
XLA Ops:
  0.0 53.2 %radiosity.1 = f32[128,128]{1,0:T(8,128)} custom-call(f32[3,4096]{1,0:T(4,128)} %positions_hbm.1, f32[2,4096]{1,0:T(2,128)} %angles_hbm.1, f32[1,4096]{1,0:T(1,128)} %bitcast.2, s32[1,4096]{1,0:T(1,128)} %bitcast.3, f32[4096,128]{1,0:T(8,128)} %b_hbm.1, s32[128,128]{1,0:T(8,128)} %visible_hbm.1, f32[128,128]{1,0:T(8,128)} %emission_hbm.1, f32[128,128]{1,0:T(8,128)} %reflect_hbm.1), custom_call_target="tpu_custom_call" | custom-call | tf_op jit(solution)/shard_map/radiosity/pallas_call | solution.py:486
  53.2 1.5 %copy.10 = f32[128,128]{1,0:T(8,128)} copy(f32[128,128]{1,0:T(8,128)} %radiosity.1) | data formatting | bytes 131072
